TPU v7x, 32 devices: a whole 2x2x4 slice. The times are simulated.
32 devices in a mesh: col: 8 (over z, x), row: 4 (over y, core).
Axes of the slice: x: 2, y: 2, z: 4, core: 2. Of those that a mesh axis runs over, the one named last changes fastest.
Arguments:
- returns: bfloat16 [4096, 2048], P(('row', 'col')), may hold values from -6 to 6
- counts: int32 [4096], P(('row', 'col')), may hold values from 0 to 4
- partner_shift: int32 [3], replicated, may hold values from 1 to 7
Outputs:
- blocks_out: float32 [4096, 2048], P('row', 'col')
- bounds: float32 [3], replicated
All inputs are finite; a program needn't handle non-finite values.
Results may differ from a plain program's by a relative error of at most 0.0003.
Values sent between devices are 32-bit elements; how exact they have to be, the bound alone decides.
No kernel may reach another device: no remote copies, remote signals or barrier semaphores. Data moves between devices by JAX's collectives and lax.ppermute only.
A program may use at most 128 MiB of HBM per device.

v0:
```python
import jax
import jax.numpy as jnp
from jax import lax
from jax.sharding import PartitionSpec as P

BW = 128
ROUNDS = 3


HIGH = lax.Precision.HIGHEST


def passed_along(block, axis, distance):
    devices = range(lax.axis_size(axis))
    route = [((i - distance) % len(devices), i) for i in devices]
    return lax.ppermute(block, axis, route)


def rotation(coupling, top):
    width = coupling.shape[0]
    zeros = jnp.zeros((width, width), jnp.float32)
    skew = jnp.concatenate(
        [jnp.concatenate([zeros, coupling], 1), jnp.concatenate([-coupling.T, zeros], 1)], 0
    )
    factor = (jnp.eye(2 * width, dtype=jnp.float32) + skew) / jnp.sqrt(1.0 + top)
    for step in range(3):
        inner = jnp.dot(factor.T, factor, precision=HIGH)
        factor = 1.5 * factor - 0.5 * jnp.dot(factor, inner, precision=HIGH)
    return factor


def move_forward(block, amount, total_bits):
    for level in range(total_bits):
        moved = passed_along(block, "col", 1 << level)
        block = jnp.where((amount >> level) % 2 == 1, moved, block)
    return block


def on_device(returns, counts, partner_shift):
    width = BW
    col_count = lax.axis_size("col")
    total_bits = max(1, (col_count - 1).bit_length())
    total_days = returns.shape[0] * col_count * lax.axis_size("row")
    weighted = returns.astype(jnp.float32) * jnp.sqrt(counts.astype(jnp.float32))[:, None]
    pair = lax.all_to_all(weighted, "col", split_axis=1, concat_axis=0, tiled=True)
    bound_list = []
    for rnd in range(ROUNDS):
        partial_gram = jnp.dot(pair.T, pair, precision=HIGH)
        gram = lax.psum(partial_gram, "row")
        cross = gram[:width, width:]
        squares = jnp.diagonal(gram)
        norms = jnp.sqrt(squares / total_days + 1e-06)
        coupling = cross / (total_days * norms[:width, None] * norms[None, width:])
        measure = jnp.sum(coupling * coupling)
        top = lax.pmax(measure, "col")
        bound_list.append(top)
        factor = rotation(coupling, top)
        rotated = jnp.dot(pair, factor, precision=HIGH)
        keep = rotated[:, :width]
        moving = rotated[:, width:]
        amount = partner_shift[rnd]
        moving = move_forward(moving, amount, total_bits)
        pair = jnp.concatenate([keep, moving], axis=1)
    return (pair, jnp.stack(bound_list))


def solution(mesh):
    placed = (P(("row", "col"), None), P(("row", "col")), P())
    return jax.shard_map(
        on_device, mesh=mesh, in_specs=placed, out_specs=(P("row", "col"), P()), check_vma=False
    )
```

profile of v0, /device:TPU:0, one launch (start us, length us, event | category | flops | bytes accessed | tf_op | source)
XLA Modules:
  0.0 375.2 jit_solution(276600851005744360)
XLA Ops:
  7.2 1.3 copy.16
  9.0 32.8 %all_to_all.19 = f32[128,8,256]{2,0,1:T(8,128)S(1)} all-to-all(f32[128,8,256]{2,0,1:T(8,128)S(1)} %copy.17), channel_id=1, replica_groups=mesh['col'=8,'row'=4] {'col'}, dimensions={1} | all-to-all | bytes 2097152 | tf_op jit(solution)/shard_map/all_to_all | solution.py:45
  41.8 2.6 convolution_bitcast_fusion
  44.5 31.1 %all-reduce.10.cloned.1.call-done = f32[256,256]{1,0:T(8,128)} async-done(((f32[256,256]{1,0:T(8,128)}), f32[256,256]{1,0:T(8,128)}) %all-reduce.10.cloned.1.call-update) | async-done | bytes 262160 | tf_op jit(solution)/shard_map/psum | solution.py:49
  75.6 2.6 gather_fusion
  78.2 1.5 multiply_reduce_fusion.2
  79.8 22.1 %pmax.21 = f32[]{:T(128)} all-reduce(f32[]{:T(128)} %get-tuple-element.10), channel_id=1, replica_groups=mesh['col'=8,'row'=4] {'col'}, use_global_device_ids=true, to_apply=%region_2.3 | all-reduce | flops 1 | bytes 8 | tf_op jit(solution)/shard_map/pmax | solution.py:55
  102.6 0.4 fusion.23
  103.1 0.6 fusion.8
  103.7 0.4 fusion.52
  104.1 0.6 fusion.7
  104.7 0.4 fusion.53
  105.1 0.6 fusion.6
  105.7 1.1 fusion.54
  106.9 0.5 copy-done
  107.5 0.6 fusion.51
  108.7 14.7 %collective-permute-done = f32[1024,128]{0,1:T(8,128)S(1)} collective-permute-done((f32[1024,128]{0,1:T(8,128)S(1)}, f32[1024,128]{0,1:T(8,128)S(1)}, u32[]{:S(2)}, u32[]{:S(2)}) %collective-permute-start) | collective-permute-done | bytes 524320 | tf_op jit(solution)/shard_map/ppermute | solution.py:16
  124.3 11.2 %collective-permute-done.1 = f32[1024,128]{0,1:T(8,128)S(1)} collective-permute-done((f32[1024,128]{0,1:T(8,128)S(1)}, f32[1024,128]{0,1:T(8,128)S(1)}, u32[]{:S(2)}, u32[]{:S(2)}) %collective-permute-start.1) | collective-permute-done | bytes 524320 | tf_op jit(solution)/shard_map/ppermute | solution.py:16
  136.3 15.9 %collective-permute-done.2 = f32[1024,128]{0,1:T(8,128)S(1)} collective-permute-done((f32[1024,128]{0,1:T(8,128)S(1)}, f32[1024,128]{0,1:T(8,128)S(1)}, u32[]{:S(2)}, u32[]{:S(2)}) %collective-permute-start.2) | collective-permute-done | bytes 524320 | tf_op jit(solution)/shard_map/ppermute | solution.py:16
  152.3 1.7 fusion.13
  154.1 28.9 %all-reduce.12.cloned.1.call-done = f32[256,256]{1,0:T(8,128)} async-done(((f32[256,256]{1,0:T(8,128)}), f32[256,256]{1,0:T(8,128)}) %all-reduce.12.cloned.1.call-update) | async-done | bytes 262160 | tf_op jit(solution)/shard_map/psum | solution.py:49
  183.1 2.6 gather_fusion.1
  185.6 1.5 multiply_reduce_fusion.1
  187.3 22.2 %pmax.22 = f32[]{:T(128)} all-reduce(f32[]{:T(128)} %get-tuple-element.8), channel_id=1, replica_groups=mesh['col'=8,'row'=4] {'col'}, use_global_device_ids=true, to_apply=%region_5.6 | all-reduce | flops 1 | bytes 8 | tf_op jit(solution)/shard_map/pmax | solution.py:55
  210.1 0.4 fusion.20
  210.5 0.6 fusion.5
  211.5 0.6 fusion.4
  212.6 0.6 fusion.3
  213.2 1.1 fusion.12
  215.0 15.8 %collective-permute-done.3 = f32[1024,128]{0,1:T(8,128)S(1)} collective-permute-done((f32[1024,128]{0,1:T(8,128)S(1)}, f32[1024,128]{0,1:T(8,128)S(1)}, u32[]{:S(2)}, u32[]{:S(2)}) %collective-permute-start.3) | collective-permute-done | bytes 524320 | tf_op jit(solution)/shard_map/ppermute | solution.py:16
  231.7 11.3 %collective-permute-done.4 = f32[1024,128]{0,1:T(8,128)S(1)} collective-permute-done((f32[1024,128]{0,1:T(8,128)S(1)}, f32[1024,128]{0,1:T(8,128)S(1)}, u32[]{:S(2)}, u32[]{:S(2)}) %collective-permute-start.4) | collective-permute-done | bytes 524320 | tf_op jit(solution)/shard_map/ppermute | solution.py:16
  243.7 16.0 %collective-permute-done.5 = f32[1024,128]{0,1:T(8,128)S(1)} collective-permute-done((f32[1024,128]{0,1:T(8,128)S(1)}, f32[1024,128]{0,1:T(8,128)S(1)}, u32[]{:S(2)}, u32[]{:S(2)}) %collective-permute-start.5) | collective-permute-done | bytes 524320 | tf_op jit(solution)/shard_map/ppermute | solution.py:16
  259.8 1.7 fusion.11
  261.5 29.1 %all-reduce.14.cloned.1.call-done = f32[256,256]{1,0:T(8,128)} async-done(((f32[256,256]{1,0:T(8,128)}), f32[256,256]{1,0:T(8,128)}) %all-reduce.14.cloned.1.call-update) | async-done | bytes 262160 | tf_op jit(solution)/shard_map/psum | solution.py:49
  290.6 2.6 gather_fusion.2
  293.2 1.5 multiply_reduce_fusion
  294.9 22.0 %pmax.23 = f32[]{:T(128)} all-reduce(f32[]{:T(128)} %get-tuple-element.6), channel_id=1, replica_groups=mesh['col'=8,'row'=4] {'col'}, use_global_device_ids=true, to_apply=%region_8.9 | all-reduce | flops 1 | bytes 8 | tf_op jit(solution)/shard_map/pmax | solution.py:55
  317.6 0.4 fusion.17
  318.0 0.6 fusion.2
  319.0 0.6 fusion.1
  319.6 0.4 fusion.58
  320.0 0.6 fusion
  320.6 1.1 fusion.10
  322.5 15.8 %collective-permute-done.6 = f32[1024,128]{0,1:T(8,128)S(1)} collective-permute-done((f32[1024,128]{0,1:T(8,128)S(1)}, f32[1024,128]{0,1:T(8,128)S(1)}, u32[]{:S(2)}, u32[]{:S(2)}) %collective-permute-start.6) | collective-permute-done | bytes 524320 | tf_op jit(solution)/shard_map/ppermute | solution.py:16
  339.2 11.2 %collective-permute-done.7 = f32[1024,128]{0,1:T(8,128)S(1)} collective-permute-done((f32[1024,128]{0,1:T(8,128)S(1)}, f32[1024,128]{0,1:T(8,128)S(1)}, u32[]{:S(2)}, u32[]{:S(2)}) %collective-permute-start.7) | collective-permute-done | bytes 524320 | tf_op jit(solution)/shard_map/ppermute | solution.py:16
  351.2 2.5 pad_maximum_fusion.7
  353.7 13.5 %collective-permute-done.8 = f32[1024,128]{0,1:T(8,128)S(1)} collective-permute-done((f32[1024,128]{0,1:T(8,128)S(1)}, f32[1024,128]{0,1:T(8,128)S(1)}, u32[]{:S(2)}, u32[]{:S(2)}) %collective-permute-start.8) | collective-permute-done | bytes 524320 | tf_op jit(solution)/shard_map/ppermute | solution.py:16
  367.3 1.3 copy.28
  (50 shorter events, 3.7 us)
Async XLA Ops:
  7.2 1.4 copy-start.1
  7.2 68.4 %all-reduce.10.cloned.1.call-start = ((), (), s32[]{:S(2)}) async-start(), calls=%async_computation.1 | async-start | bytes 524288 | tf_op jit(solution)/shard_map/psum | solution.py:49
  44.4 138.6 %all-reduce.12.cloned.1.call-start = ((), (), s32[]{:S(2)}) async-start(), calls=%async_computation.2 | async-start | bytes 524288 | tf_op jit(solution)/shard_map/psum | solution.py:49
  106.8 0.7 copy-start
  106.9 16.5 %collective-permute-start = (f32[1024,128]{0,1:T(8,128)S(1)}, f32[1024,128]{0,1:T(8,128)S(1)}, u32[]{:S(2)}, u32[]{:S(2)}) collective-permute-start(f32[1024,128]{0,1:T(8,128)S(1)} %slice.80), channel_id=1, source_target_pairs={{28,0},{0,4},{4,8},{8,12},{12,16},{16,20},{20,24},{24,28},{29,1},{... | collective-permute-start | bytes 1572872 | tf_op jit(solution)/shard_map/ppermute | solution.py:16
  123.5 12.0 %collective-permute-start.1 = (f32[1024,128]{0,1:T(8,128)S(1)}, f32[1024,128]{0,1:T(8,128)S(1)}, u32[]{:S(2)}, u32[]{:S(2)}) collective-permute-start(f32[1024,128]{0,1:T(8,128)S(1)} %get-tuple-element.17), channel_id=1, source_target_pairs={{24,0},{28,4},{0,8},{4,12},{8,16},{12,20},{16,24},{20,28},{25,1},{... | collective-permute-start | bytes 1572872 | tf_op jit(solution)/shard_map/ppermute | solution.py:16
  135.6 16.7 %collective-permute-start.2 = (f32[1024,128]{0,1:T(8,128)S(1)}, f32[1024,128]{0,1:T(8,128)S(1)}, u32[]{:S(2)}, u32[]{:S(2)}) collective-permute-start(f32[1024,128]{0,1:T(8,128)S(1)} %broadcast_select_fusion.7), channel_id=1, source_target_pairs={{16,0},{20,4},{24,8},{28,12},{0,16},{4,20},{8,24},{12,28},{17,1},{... | collective-permute-start | bytes 1572872 | tf_op jit(solution)/shard_map/ppermute | solution.py:16
  154.1 136.5 %all-reduce.14.cloned.1.call-start = ((), (), s32[]{:S(2)}) async-start(), calls=%async_computation.3 | async-start | bytes 524288 | tf_op jit(solution)/shard_map/psum | solution.py:49
  214.3 16.5 %collective-permute-start.3 = (f32[1024,128]{0,1:T(8,128)S(1)}, f32[1024,128]{0,1:T(8,128)S(1)}, u32[]{:S(2)}, u32[]{:S(2)}) collective-permute-start(f32[1024,128]{0,1:T(8,128)S(1)} %slice.83), channel_id=1, source_target_pairs={{28,0},{0,4},{4,8},{8,12},{12,16},{16,20},{20,24},{24,28},{29,1},{... | collective-permute-start | bytes 1572872 | tf_op jit(solution)/shard_map/ppermute | solution.py:16
  231.0 12.0 %collective-permute-start.4 = (f32[1024,128]{0,1:T(8,128)S(1)}, f32[1024,128]{0,1:T(8,128)S(1)}, u32[]{:S(2)}, u32[]{:S(2)}) collective-permute-start(f32[1024,128]{0,1:T(8,128)S(1)} %get-tuple-element.15), channel_id=1, source_target_pairs={{24,0},{28,4},{0,8},{4,12},{8,16},{12,20},{16,24},{20,28},{25,1},{... | collective-permute-start | bytes 1572872 | tf_op jit(solution)/shard_map/ppermute | solution.py:16
  243.0 16.7 %collective-permute-start.5 = (f32[1024,128]{0,1:T(8,128)S(1)}, f32[1024,128]{0,1:T(8,128)S(1)}, u32[]{:S(2)}, u32[]{:S(2)}) collective-permute-start(f32[1024,128]{0,1:T(8,128)S(1)} %broadcast_select_fusion.4), channel_id=1, source_target_pairs={{16,0},{20,4},{24,8},{28,12},{0,16},{4,20},{8,24},{12,28},{17,1},{... | collective-permute-start | bytes 1572872 | tf_op jit(solution)/shard_map/ppermute | solution.py:16
  321.8 16.5 %collective-permute-start.6 = (f32[1024,128]{0,1:T(8,128)S(1)}, f32[1024,128]{0,1:T(8,128)S(1)}, u32[]{:S(2)}, u32[]{:S(2)}) collective-permute-start(f32[1024,128]{0,1:T(8,128)S(1)} %slice.86), channel_id=1, source_target_pairs={{28,0},{0,4},{4,8},{8,12},{12,16},{16,20},{20,24},{24,28},{29,1},{... | collective-permute-start | bytes 1572872 | tf_op jit(solution)/shard_map/ppermute | solution.py:16
  338.4 12.0 %collective-permute-start.7 = (f32[1024,128]{0,1:T(8,128)S(1)}, f32[1024,128]{0,1:T(8,128)S(1)}, u32[]{:S(2)}, u32[]{:S(2)}) collective-permute-start(f32[1024,128]{0,1:T(8,128)S(1)} %get-tuple-element.13), channel_id=1, source_target_pairs={{24,0},{28,4},{0,8},{4,12},{8,16},{12,20},{16,24},{20,28},{25,1},{... | collective-permute-start | bytes 1572872 | tf_op jit(solution)/shard_map/ppermute | solution.py:16
  350.5 16.7 %collective-permute-start.8 = (f32[1024,128]{0,1:T(8,128)S(1)}, f32[1024,128]{0,1:T(8,128)S(1)}, u32[]{:S(2)}, u32[]{:S(2)}) collective-permute-start(f32[1024,128]{0,1:T(8,128)S(1)} %broadcast_select_fusion.1), channel_id=1, source_target_pairs={{16,0},{20,4},{24,8},{28,12},{0,16},{4,20},{8,24},{12,28},{17,1},{... | collective-permute-start | bytes 1572872 | tf_op jit(solution)/shard_map/ppermute | solution.py:16
Sparse Core Ops, SparseCore 0:
  44.5 30.9 all-reduce.9
  154.2 28.7 all-reduce.11
  261.7 28.9 all-reduce.13
where the time goes:
time: 376 us; the launch traced here: 375 us
  waiting for transfers between devices  215 us (57%)
  blocking collectives  99.1 us (26%)
  between operations  22.2 us (6%)
  matrix products  18.5 us (5%)
  local copies, waits for them, and re-layouts  12.2 us (3%)
  other arithmetic  8.14 us (2%)
    ppermute x9, waiting for transfers between devices, passed_along(): return lax.ppermute(block, axis, route)  125 us
    psum x3, waiting for transfers between devices, on_device(): gram = lax.psum(partial_gram, 'row')  89.1 us
    pmax x3, blocking collectives, on_device(): top = lax.pmax(measure, 'col')  66.2 us
    all_to_all x1, blocking collectives, on_device(): lax.all_to_all(weighted, 'col', split_axis=1, concat_axis=0, tiled=True)  32.8 us
    gather x3, local copies, waits for them, and re-layouts, on_device(): squares = jnp.diagonal(gram)  7.7 us
  transfers between devices with their start and end apart: 12, of which 12 were waited for; matrix products, arithmetic and copies ran while one was open for 1% of the time, Pallas kernels for 0%

commit v1 on v0

v1 whole, which is shorter than its diff:
```python
import jax
import jax.numpy as jnp
from jax import lax
from jax.sharding import PartitionSpec as P

BW = 128
ROUNDS = 3
RADIX = 8
HIGH = lax.Precision.HIGH


def dot(a, b):
    return jnp.dot(a, b, precision=HIGH)


def forward(x, hop):
    n = lax.axis_size("col")
    return lax.ppermute(x, "col", [(i, (i + hop) % n) for i in range(n)])


def swapped(x, axis, mask):
    return lax.ppermute(x, axis, [(i, i ^ mask) for i in range(lax.axis_size(axis))])


def row_sum(x):
    parts = [x] + [swapped(x, "row", m) for m in range(1, lax.axis_size("row"))]
    while len(parts) > 1:
        parts = [parts[i] + parts[i + 1] for i in range(0, len(parts), 2)]
    return parts[0]


def col_max(x):
    mask = 1
    while mask < lax.axis_size("col"):
        x = jnp.maximum(x, swapped(x, "col", mask))
        mask *= 2
    return x


def to_pairs(weighted):
    n = lax.axis_size("col")
    if n > RADIX:
        return lax.all_to_all(weighted, "col", split_axis=1, concat_axis=0, tiled=True)
    me = lax.axis_index("col")
    days, width = weighted.shape[0], weighted.shape[1] // n
    pair = jnp.zeros((days * n, width), jnp.float32)
    for hop in [4, 3, 5, 2, 6, 1, 7, 0]:
        if hop >= n:
            continue
        block = lax.dynamic_slice(weighted, (0, (me + hop) % n * width), (days, width))
        block = forward(block, hop) if hop else block
        pair = lax.dynamic_update_slice(pair, block, ((me - hop) % n * days, 0))
    return pair


def polar(m, top):
    eye = jnp.eye(m.shape[0], dtype=jnp.float32)
    square = 1.0 / (1.0 + top)
    gram = square * (eye + m)
    t0 = 1.5 * eye - 0.5 * gram
    gram = dot(gram, dot(t0, t0))
    t1 = 1.5 * eye - 0.5 * gram
    gram = dot(gram, dot(t1, t1))
    t2 = 1.5 * eye - 0.5 * gram
    return jnp.sqrt(square) * dot(dot(t0, t1), t2)


def on_device(returns, counts, partner_shift):
    n = lax.axis_size("col")
    days = returns.shape[0] * n * lax.axis_size("row")
    weighted = returns.astype(jnp.float32) * jnp.sqrt(counts.astype(jnp.float32))[:, None]
    pair = to_pairs(weighted)
    first, second = pair[:, :BW], pair[:, BW:]
    strides = [1]
    while strides[-1] * RADIX < n:
        strides.append(strides[-1] * RADIX)
    lowest = 1 if len(strides) == 1 else 0
    bounds = []
    for rnd in range(ROUNDS):
        cross = dot(first.T, second)
        squares = jnp.stack([jnp.sum(first * first, 0), jnp.sum(second * second, 0)])
        summed = row_sum(jnp.concatenate([cross, squares, jnp.zeros((6, BW), jnp.float32)], 0))
        norms = jnp.sqrt(summed[BW:BW + 2] / days + 1e-06)
        coupling = summed[:BW] / (days * norms[0][:, None] * norms[1][None, :])
        measure = jnp.sum(coupling * coupling)
        mixed = dot(first, coupling) + second

        def move(hop, first, second, mixed, coupling, measure):
            there = forward(coupling, hop) if hop else coupling
            mixed = forward(mixed, hop) if hop else mixed
            top = col_max(jnp.broadcast_to(measure, (8, BW)))[0, 0]
            kept = dot(first - dot(second, coupling.T), polar(dot(coupling, coupling.T), top))
            return kept, mixed, polar(dot(there.T, there), top), top

        amount = partner_shift[rnd]
        branches = [
            lambda *a, hop=hop: move(hop, *a) for hop in range(lowest, min(n, RADIX))
        ]
        first, mixed, factor, top = lax.switch(
            amount % RADIX - lowest, branches, first, second, mixed, coupling, measure
        )
        for stride in strides[1:]:
            routes = [lambda *a: a] + [
                lambda *a, hop=hop: tuple(forward(v, hop * stride) for v in a)
                for hop in range(1, min(RADIX, n // stride))
            ]
            mixed, factor = lax.switch(amount // stride % RADIX, routes, mixed, factor)
        second = dot(mixed, factor)
        bounds.append(top)
    return jnp.concatenate([first, second], 1), jnp.stack(bounds)


def solution(mesh):
    placed = (P(("row", "col"), None), P(("row", "col")), P())
    return jax.shard_map(
        on_device, mesh=mesh, in_specs=placed, out_specs=(P("row", "col"), P()), check_vma=False
    )
```

time: 376 us -> 183 us (0.49)
  waiting for transfers between devices: 215 us -> 75.6 us
  blocking collectives: 99.1 us -> 0 us
  starting transfers between devices: 0.69 us -> 44.7 us
  loops' own time: 0 us -> 18.8 us
  between operations: 22.2 us -> 7.27 us
    psum x3 -> x0, waiting for transfers between devices: 89.1 us -> none  [on_device(): gram = lax.psum(partial_gram, 'row')]
    pmax x3 -> x0, blocking collectives: 66.2 us -> none  [on_device(): top = lax.pmax(measure, 'col')]
    ppermute x9 -> x31, waiting for transfers between devices: 125 us -> 75.6 us  [the longest x18 66.2 us: swapped(): lax.ppermute(x, axis, [(i, i ^ mask) for i in range(lax.axis_size(axis))])]
    ppermute x9 -> x31, starting transfers between devices: 0.56 us -> 44.7 us  [the longest x13 28.3 us: forward(): return lax.ppermute(x, 'col', [(i, (i + hop) % n) for i in range(n)])]
    all_to_all x1 -> x0, blocking collectives: 32.8 us -> none  [on_device(): lax.all_to_all(weighted, 'col', split_axis=1, concat_axis=0, tiled=True)]
    another operation x0 -> x3, loops' own time: none -> 18.8 us  [on_device(): lax.switch(amount % RADIX - lowest, branches, first, second, mixed, coupl...]
    gather x3 -> x0, local copies, waits for them, and re-layouts: 7.7 us -> none  [on_device(): squares = jnp.diagonal(gram)]
    max x0 -> x9, other arithmetic: none -> 3.92 us  [col_max(): x = jnp.maximum(x, swapped(x, 'col', mask))]
  transfers between devices with their start and end apart: 12 -> 31, of which waited for: 12 -> 16; matrix products, arithmetic and copies ran while one was open for 1% -> 9% of each run, Pallas kernels for 0% -> 0%
where the time goes in v1:
time: 183 us
  waiting for transfers between devices  75.6 us (41%)
  starting transfers between devices  44.7 us (24%)
  loops' own time  18.8 us (10%)
  matrix products  17.3 us (9%)
  other arithmetic  10.8 us (6%)
  local copies, waits for them, and re-layouts  9.02 us (5%)
  between operations  7.27 us (4%)
    ppermute x18, waiting for transfers between devices, swapped(): lax.ppermute(x, axis, [(i, i ^ mask) for i in range(lax.axis_size(axis))])  66.2 us
    ppermute x13, starting transfers between devices, forward(): return lax.ppermute(x, 'col', [(i, (i + hop) % n) for i in range(n)])  28.3 us
    another operation x3, loops' own time, on_device(): lax.switch(amount % RADIX - lowest, branches, first, second, mixed, coupl...  18.8 us
    dot_general x56, matrix products, dot(): return jnp.dot(a, b, precision=HIGH)  16.9 us
    ppermute x18, starting transfers between devices, swapped(): lax.ppermute(x, axis, [(i, i ^ mask) for i in range(lax.axis_size(axis))])  16.3 us
    ppermute x13, waiting for transfers between devices, forward(): return lax.ppermute(x, 'col', [(i, (i + hop) % n) for i in range(n)])  9.4 us
    max x9, other arithmetic, col_max(): x = jnp.maximum(x, swapped(x, 'col', mask))  3.92 us
  transfers between devices with their start and end apart: 31, of which 16 were waited for; matrix products, arithmetic and copies ran while one was open for 9% of the time, Pallas kernels for 0%

profile of v1, /device:TPU:0, one launch (start us, length us, event | category | flops | bytes accessed | tf_op | source)
XLA Modules:
  0.0 183.5 jit_solution(12831939250800139370)
XLA Ops:
  1.4 1.2 convert_multiply_fusion
  2.7 4.1 %collective-permute-start.105 = (f32[128,256]{1,0:T(8,128)S(1)}, f32[128,256]{1,0:T(8,128)S(1)}, u32[]{:S(2)}, u32[]{:S(2)}) collective-permute-start(f32[128,256]{1,0:T(8,128)S(1)} %get-tuple-element.454), channel_id=1, source_target_pairs={{0,16},{4,20},{8,24},{12,28},{16,0},{20,4},{24,8},{28,12},{1,17},{... | collective-permute-start | bytes 393224 | tf_op jit(solution)/shard_map/ppermute | solution.py:18
  6.8 2.5 %collective-permute-start.106 = (f32[128,256]{1,0:T(8,128)S(1)}, f32[128,256]{1,0:T(8,128)}, u32[]{:S(2)}, u32[]{:S(2)}) collective-permute-start(f32[128,256]{1,0:T(8,128)S(1)} %get-tuple-element.453), channel_id=1, source_target_pairs={{0,12},{4,16},{8,20},{12,24},{16,28},{20,0},{24,4},{28,8},{1,13},{... | collective-permute-start | bytes 393224 | tf_op jit(solution)/shard_map/ppermute | solution.py:18
  9.3 1.3 collective-permute-start.107
  10.6 1.6 collective-permute-start.108
  12.2 2.2 %collective-permute-start.109 = (f32[128,256]{1,0:T(8,128)S(1)}, f32[128,256]{1,0:T(8,128)S(1)}, u32[]{:S(2)}, u32[]{:S(2)}) collective-permute-start(f32[128,256]{1,0:T(8,128)S(1)} %get-tuple-element.450), channel_id=1, source_target_pairs={{0,24},{4,28},{8,0},{12,4},{16,8},{20,12},{24,16},{28,20},{1,25},{... | collective-permute-start | bytes 393224 | tf_op jit(solution)/shard_map/ppermute | solution.py:18
  14.5 7.9 %collective-permute-done.105 = f32[128,256]{1,0:T(8,128)S(1)} collective-permute-done((f32[128,256]{1,0:T(8,128)S(1)}, f32[128,256]{1,0:T(8,128)S(1)}, u32[]{:S(2)}, u32[]{:S(2)}) %collective-permute-start.105) | collective-permute-done | bytes 131104 | tf_op jit(solution)/shard_map/ppermute | solution.py:18
  23.1 0.8 copy-done.1
  24.0 4.8 %collective-permute-start.111 = (f32[128,256]{1,0:T(8,128)S(1)}, f32[128,256]{1,0:T(8,128)S(1)}, u32[]{:S(2)}, u32[]{:S(2)}) collective-permute-start(f32[128,256]{1,0:T(8,128)S(1)} %get-tuple-element.448), channel_id=1, source_target_pairs={{0,28},{4,0},{8,4},{12,8},{16,12},{20,16},{24,20},{28,24},{1,29},{... | collective-permute-start | bytes 393224 | tf_op jit(solution)/shard_map/ppermute | solution.py:18
  28.8 0.9 constant_dynamic-update-slice_fusion.5
  29.8 1.0 collective-permute-done.110
  32.3 1.9 %collective-permute-start.113 = (f32[136,128]{1,0:T(8,128)S(1)}, f32[136,128]{1,0:T(8,128)S(1)}, u32[]{:S(2)}, u32[]{:S(2)}) collective-permute-start(f32[136,128]{1,0:T(8,128)S(1)} %maximum_maximum_fusion), channel_id=1, source_target_pairs={{0,2},{1,3},{2,0},{3,1},{4,6},{5,7},{6,4},{7,5},{8,10},{9,11},{10,... | collective-permute-start | bytes 208904 | tf_op jit(solution)/shard_map/ppermute | solution.py:22
  37.0 1.4 collective-permute-done.114
  38.9 31.5 %conditional.3 = (f32[1024,128]{1,0:T(8,128)S(1)}, f32[1024,128]{1,0:T(8,128)}, f32[128,128]{1,0:T(8,128)S(1)}, f32[1,128]{1,0:T(1,128)S(1)}, f32[1]{0:T(128)}) conditional(s32[]{:T(128)} %clamp.11, (f32[1024,128]{1,0:T(8,128)S(1)}, f32[128,128]{1,0:T(8,128)S(1)}, f32[1024,128]{1,0:T(8,128)S(1)}, ...), branch_computations={%region_2.0_spmd, %region_5.0_spmd, %region_8.0_spmd, %region_11.0... | conditional | flops 378867584 | bytes 9196344 | solution.py:99
  43.3 0.7 multiply_reduce_fusion.11
  44.7 3.6 %collective-permute-done.25 = f32[8,128]{1,0:T(8,128)S(1)} collective-permute-done((f32[8,128]{1,0:T(8,128)S(1)}, f32[8,128]{1,0:T(8,128)S(1)}, u32[]{:S(2)}, u32[]{:S(2)}) %collective-permute-start.25) | collective-permute-done | bytes 4128 | tf_op jit(solution)/shard_map/cond/branch_5_fun/ppermute | solution.py:22
  49.0 3.7 %collective-permute-start.29 = (f32[128,128]{1,0:T(8,128)S(1)}, f32[128,128]{1,0:T(8,128)S(1)}, u32[]{:S(2)}, u32[]{:S(2)}) collective-permute-start(f32[128,128]{1,0:T(8,128)S(1)} %get-tuple-element.321), channel_id=1, source_target_pairs={{0,24},{4,28},{8,0},{12,4},{16,8},{20,12},{24,16},{28,20},{1,25},{... | collective-permute-start | bytes 196616 | tf_op jit(solution)/shard_map/cond/branch_5_fun/ppermute | solution.py:18
  52.8 2.0 %collective-permute-start.28 = (f32[1024,128]{1,0:T(8,128)S(1)}, f32[1024,128]{1,0:T(8,128)}, u32[]{:S(2)}, u32[]{:S(2)}) collective-permute-start(f32[1024,128]{1,0:T(8,128)S(1)} %add.353), channel_id=1, source_target_pairs={{0,24},{4,28},{8,0},{12,4},{16,8},{20,12},{24,16},{28,20},{1,25},{... | collective-permute-start | bytes 1572872 | tf_op jit(solution)/shard_map/cond/branch_5_fun/ppermute | solution.py:18
  55.9 10.0 %collective-permute-done.27 = f32[8,128]{1,0:T(8,128)S(1)} collective-permute-done((f32[8,128]{1,0:T(8,128)S(1)}, f32[8,128]{1,0:T(8,128)S(1)}, u32[]{:S(2)}, u32[]{:S(2)}) %collective-permute-start.27) | collective-permute-done | bytes 4128 | tf_op jit(solution)/shard_map/cond/branch_5_fun/ppermute | solution.py:22
  70.5 1.4 multiply_reduce_fusion.36
  72.6 1.6 collective-permute-start.116
  76.6 0.7 collective-permute-done.116
  77.2 1.1 collective-permute-done.117
  79.0 50.0 %conditional.4 = (f32[1024,128]{1,0:T(8,128)S(1)}, f32[1024,128]{1,0:T(8,128)}, f32[128,128]{1,0:T(8,128)S(1)}, f32[1,128]{1,0:T(1,128)S(1)}, f32[1]{0:T(128)}) conditional(s32[]{:T(128)} %clamp.10, (f32[1024,128]{1,0:T(8,128)S(1)}, f32[128,128]{1,0:T(8,128)S(1)}, f32[1024,128]{1,0:T(8,128)S(1)}, ...), branch_computations={%region_24.0_spmd, %region_27.0_spmd, %region_30.33_spmd, %region_... | conditional | flops 378867584 | bytes 9196344 | solution.py:99
  79.0 0.7 multiply_reduce_fusion.21
  79.7 0.7 broadcast_in_dim.55
  80.4 1.8 collective-permute-start.50
  82.2 1.9 %collective-permute-done.50 = f32[8,128]{1,0:T(8,128)S(1)} collective-permute-done((f32[8,128]{1,0:T(8,128)S(1)}, f32[8,128]{1,0:T(8,128)S(1)}, u32[]{:S(2)}, u32[]{:S(2)}) %collective-permute-start.50) | collective-permute-done | bytes 4128 | tf_op jit(solution)/shard_map/cond/branch_3_fun/ppermute | solution.py:22
  84.0 0.7 broadcast_maximum_fusion.10
  84.7 1.8 collective-permute-start.51
  86.5 1.7 collective-permute-start.54
  88.2 1.3 collective-permute-start.53
  89.6 0.7 fusion.1477
  90.2 2.2 %collective-permute-start.52 = (f32[8,128]{1,0:T(8,128)S(1)}, f32[8,128]{1,0:T(8,128)S(1)}, u32[]{:S(2)}, u32[]{:S(2)}) collective-permute-start(f32[8,128]{1,0:T(8,128)S(1)} %fusion.1477), channel_id=1, source_target_pairs={{0,16},{4,20},{8,24},{12,28},{16,0},{20,4},{24,8},{28,12},{1,17},{... | collective-permute-start | bytes 12296 | tf_op jit(solution)/shard_map/cond/branch_3_fun/ppermute | solution.py:22
  92.8 21.8 %collective-permute-done.52 = f32[8,128]{1,0:T(8,128)S(1)} collective-permute-done((f32[8,128]{1,0:T(8,128)S(1)}, f32[8,128]{1,0:T(8,128)S(1)}, u32[]{:S(2)}, u32[]{:S(2)}) %collective-permute-start.52) | collective-permute-done | bytes 4128 | tf_op jit(solution)/shard_map/cond/branch_3_fun/ppermute | solution.py:22
  128.9 1.4 multiply_reduce_fusion.35
  131.1 1.6 collective-permute-start.119
  135.0 0.8 collective-permute-done.119
  135.7 1.1 collective-permute-done.120
  137.5 40.4 %conditional.5 = (f32[1024,128]{1,0:T(8,128)}, f32[128,128]{1,0:T(8,128)S(1)}, f32[1]{0:T(128)}, f32[1024,128]{0,1:T(8,128)S(1)}) conditional(s32[]{:T(128)} %clamp.9, (f32[1024,128]{1,0:T(8,128)S(1)}, f32[128,128]{1,0:T(8,128)S(1)}, f32[1024,128]{1,0:T(8,128)S(1)}, f32[1024,128]{1,0:T(8,128)S(1)}) %tuple.129, ...), branch_computations={%region_46.48_spmd, %region_48.50_spmd, %region_50.52_spmd, %regio... | conditional | flops 378605568 | bytes 9195824 | solution.py:99
  138.8 1.8 collective-permute-start.85
  140.6 1.9 %collective-permute-done.85 = f32[8,128]{1,0:T(8,128)S(1)} collective-permute-done((f32[8,128]{1,0:T(8,128)S(1)}, f32[8,128]{1,0:T(8,128)S(1)}, u32[]{:S(2)}, u32[]{:S(2)}) %collective-permute-start.85) | collective-permute-done | bytes 4128 | tf_op jit(solution)/shard_map/cond/branch_3_fun/ppermute | solution.py:22
  143.2 3.0 %collective-permute-start.89 = (f32[128,128]{1,0:T(8,128)S(1)}, f32[128,128]{1,0:T(8,128)S(1)}, u32[]{:S(2)}, u32[]{:S(2)}) collective-permute-start(f32[128,128]{1,0:T(8,128)S(1)} %get-tuple-element.369), channel_id=1, source_target_pairs={{0,16},{4,20},{8,24},{12,28},{16,0},{20,4},{24,8},{28,12},{1,17},{... | collective-permute-start | bytes 196616 | tf_op jit(solution)/shard_map/cond/branch_3_fun/ppermute | solution.py:18
  147.4 2.5 %collective-permute-start.87 = (f32[8,128]{1,0:T(8,128)S(1)}, f32[8,128]{1,0:T(8,128)S(1)}, u32[]{:S(2)}, u32[]{:S(2)}) collective-permute-start(f32[8,128]{1,0:T(8,128)S(1)} %fusion.1484), channel_id=1, source_target_pairs={{0,16},{4,20},{8,24},{12,28},{16,0},{20,4},{24,8},{28,12},{1,17},{... | collective-permute-start | bytes 12296 | tf_op jit(solution)/shard_map/cond/branch_3_fun/ppermute | solution.py:22
  150.4 21.5 %collective-permute-done.87 = f32[8,128]{1,0:T(8,128)S(1)} collective-permute-done((f32[8,128]{1,0:T(8,128)S(1)}, f32[8,128]{1,0:T(8,128)S(1)}, u32[]{:S(2)}, u32[]{:S(2)}) %collective-permute-start.87) | collective-permute-done | bytes 4128 | tf_op jit(solution)/shard_map/cond/branch_3_fun/ppermute | solution.py:22
  177.9 1.5 fusion.1031
  179.4 1.3 copy.6
  180.7 2.5 %pad_maximum_fusion.1 = f32[3]{0:T(128)} fusion(f32[1]{0:T(128)} %get-tuple-element.412, f32[1]{0:T(128)} %get-tuple-element.411, f32[1]{0:T(128)} %get-tuple-element.410), kind=kLoop, calls=%fused_computation.1313 | loop fusion | flops 6 | bytes 24 | tf_op jit(solution)/shard_map/stack | solution.py:110
  (137 shorter events, 24.8 us)
Async XLA Ops:
  0.7 0.7 copy-start.3
  2.7 19.7 %collective-permute-start.105 = (f32[128,256]{1,0:T(8,128)S(1)}, f32[128,256]{1,0:T(8,128)S(1)}, u32[]{:S(2)}, u32[]{:S(2)}) collective-permute-start(f32[128,256]{1,0:T(8,128)S(1)} %get-tuple-element.454), channel_id=1, source_target_pairs={{0,16},{4,20},{8,24},{12,28},{16,0},{20,4},{24,8},{28,12},{1,17},{... | collective-permute-start | bytes 393224 | tf_op jit(solution)/shard_map/ppermute | solution.py:18
  6.8 17.2 %collective-permute-start.106 = (f32[128,256]{1,0:T(8,128)S(1)}, f32[128,256]{1,0:T(8,128)}, u32[]{:S(2)}, u32[]{:S(2)}) collective-permute-start(f32[128,256]{1,0:T(8,128)S(1)} %get-tuple-element.453), channel_id=1, source_target_pairs={{0,12},{4,16},{8,20},{12,24},{16,28},{20,0},{24,4},{28,8},{1,13},{... | collective-permute-start | bytes 393224 | tf_op jit(solution)/shard_map/ppermute | solution.py:18
  9.3 20.4 %collective-permute-start.107 = (f32[128,256]{1,0:T(8,128)S(1)}, f32[128,256]{1,0:T(8,128)S(1)}, u32[]{:S(2)}, u32[]{:S(2)}) collective-permute-start(f32[128,256]{1,0:T(8,128)S(1)} %get-tuple-element.452), channel_id=1, source_target_pairs={{0,20},{4,24},{8,28},{12,0},{16,4},{20,8},{24,12},{28,16},{1,21},{... | collective-permute-start | bytes 393224 | tf_op jit(solution)/shard_map/ppermute | solution.py:18
  10.6 19.1 %collective-permute-start.108 = (f32[128,256]{1,0:T(8,128)S(1)}, f32[128,256]{1,0:T(8,128)S(1)}, u32[]{:S(2)}, u32[]{:S(2)}) collective-permute-start(f32[128,256]{1,0:T(8,128)S(1)} %get-tuple-element.451), channel_id=1, source_target_pairs={{0,8},{4,12},{8,16},{12,20},{16,24},{20,28},{24,0},{28,4},{1,9},{5... | collective-permute-start | bytes 393224 | tf_op jit(solution)/shard_map/ppermute | solution.py:18
  12.2 17.6 %collective-permute-start.109 = (f32[128,256]{1,0:T(8,128)S(1)}, f32[128,256]{1,0:T(8,128)S(1)}, u32[]{:S(2)}, u32[]{:S(2)}) collective-permute-start(f32[128,256]{1,0:T(8,128)S(1)} %get-tuple-element.450), channel_id=1, source_target_pairs={{0,24},{4,28},{8,0},{12,4},{16,8},{20,12},{24,16},{28,20},{1,25},{... | collective-permute-start | bytes 393224 | tf_op jit(solution)/shard_map/ppermute | solution.py:18
  22.4 0.7 copy-start
  23.1 7.8 %collective-permute-start.110 = (f32[128,256]{1,0:T(8,128)S(1)}, f32[128,256]{1,0:T(8,128)S(1)}, u32[]{:S(2)}, u32[]{:S(2)}) collective-permute-start(f32[128,256]{1,0:T(8,128)S(1)} %get-tuple-element.449), channel_id=1, source_target_pairs={{0,4},{4,8},{8,12},{12,16},{16,20},{20,24},{24,28},{28,0},{1,5},{5... | collective-permute-start | bytes 393224 | tf_op jit(solution)/shard_map/ppermute | solution.py:18
  23.1 0.9 copy-start.1
  24.0 7.3 %collective-permute-start.111 = (f32[128,256]{1,0:T(8,128)S(1)}, f32[128,256]{1,0:T(8,128)S(1)}, u32[]{:S(2)}, u32[]{:S(2)}) collective-permute-start(f32[128,256]{1,0:T(8,128)S(1)} %get-tuple-element.448), channel_id=1, source_target_pairs={{0,28},{4,0},{8,4},{12,8},{16,12},{20,16},{24,20},{28,24},{1,29},{... | collective-permute-start | bytes 393224 | tf_op jit(solution)/shard_map/ppermute | solution.py:18
  32.1 2.2 %copy-start.2 = (s32[3]{0:T(128)S(1)}, s32[3]{0:T(128)}, u32[]{:S(2)}) copy-start(s32[3]{0:T(128)} %param.26) | copy-start | bytes 40
  32.2 4.7 %collective-permute-start.112 = (f32[136,128]{1,0:T(8,128)S(1)}, f32[136,128]{1,0:T(8,128)S(1)}, u32[]{:S(2)}, u32[]{:S(2)}) collective-permute-start(f32[136,128]{1,0:T(8,128)S(1)} %maximum_maximum_fusion), channel_id=1, source_target_pairs={{0,1},{1,0},{2,3},{3,2},{4,5},{5,4},{6,7},{7,6},{8,9},{9,8},{10,11... | collective-permute-start | bytes 208904 | tf_op jit(solution)/shard_map/ppermute | solution.py:22
  32.3 4.7 %collective-permute-start.113 = (f32[136,128]{1,0:T(8,128)S(1)}, f32[136,128]{1,0:T(8,128)S(1)}, u32[]{:S(2)}, u32[]{:S(2)}) collective-permute-start(f32[136,128]{1,0:T(8,128)S(1)} %maximum_maximum_fusion), channel_id=1, source_target_pairs={{0,2},{1,3},{2,0},{3,1},{4,6},{5,7},{6,4},{7,5},{8,10},{9,11},{10,... | collective-permute-start | bytes 208904 | tf_op jit(solution)/shard_map/ppermute | solution.py:22
  34.2 4.1 %collective-permute-start.114 = (f32[136,128]{1,0:T(8,128)S(1)}, f32[136,128]{1,0:T(8,128)S(1)}, u32[]{:S(2)}, u32[]{:S(2)}) collective-permute-start(f32[136,128]{1,0:T(8,128)S(1)} %maximum_maximum_fusion), channel_id=1, source_target_pairs={{0,3},{1,2},{2,1},{3,0},{4,7},{5,6},{6,5},{7,4},{8,11},{9,10},{10,... | collective-permute-start | bytes 208904 | tf_op jit(solution)/shard_map/ppermute | solution.py:22
  44.6 3.7 %collective-permute-start.25 = (f32[8,128]{1,0:T(8,128)S(1)}, f32[8,128]{1,0:T(8,128)S(1)}, u32[]{:S(2)}, u32[]{:S(2)}) collective-permute-start(f32[8,128]{1,0:T(8,128)S(1)} %broadcast_in_dim.50), channel_id=1, source_target_pairs={{0,4},{4,0},{8,12},{12,8},{16,20},{20,16},{24,28},{28,24},{1,5},{5... | collective-permute-start | bytes 12296 | tf_op jit(solution)/shard_map/cond/branch_5_fun/ppermute | solution.py:22
  48.9 5.9 %collective-permute-start.26 = (f32[8,128]{1,0:T(8,128)S(1)}, f32[8,128]{1,0:T(8,128)S(1)}, u32[]{:S(2)}, u32[]{:S(2)}) collective-permute-start(f32[8,128]{1,0:T(8,128)S(1)} %broadcast_maximum_fusion.5), channel_id=1, source_target_pairs={{0,8},{4,12},{8,0},{12,4},{16,24},{20,28},{24,16},{28,20},{1,9},{5... | collective-permute-start | bytes 12296 | tf_op jit(solution)/shard_map/cond/branch_5_fun/ppermute | solution.py:22
  49.0 19.9 %collective-permute-start.29 = (f32[128,128]{1,0:T(8,128)S(1)}, f32[128,128]{1,0:T(8,128)S(1)}, u32[]{:S(2)}, u32[]{:S(2)}) collective-permute-start(f32[128,128]{1,0:T(8,128)S(1)} %get-tuple-element.321), channel_id=1, source_target_pairs={{0,24},{4,28},{8,0},{12,4},{16,8},{20,12},{24,16},{28,20},{1,25},{... | collective-permute-start | bytes 196616 | tf_op jit(solution)/shard_map/cond/branch_5_fun/ppermute | solution.py:18
  52.8 17.5 %collective-permute-start.28 = (f32[1024,128]{1,0:T(8,128)S(1)}, f32[1024,128]{1,0:T(8,128)}, u32[]{:S(2)}, u32[]{:S(2)}) collective-permute-start(f32[1024,128]{1,0:T(8,128)S(1)} %add.353), channel_id=1, source_target_pairs={{0,24},{4,28},{8,0},{12,4},{16,8},{20,12},{24,16},{28,20},{1,25},{... | collective-permute-start | bytes 1572872 | tf_op jit(solution)/shard_map/cond/branch_5_fun/ppermute | solution.py:18
  55.4 10.4 %collective-permute-start.27 = (f32[8,128]{1,0:T(8,128)S(1)}, f32[8,128]{1,0:T(8,128)S(1)}, u32[]{:S(2)}, u32[]{:S(2)}) collective-permute-start(f32[8,128]{1,0:T(8,128)S(1)} %fusion.1472), channel_id=1, source_target_pairs={{0,16},{4,20},{8,24},{12,28},{16,0},{20,4},{24,8},{28,12},{1,17},{... | collective-permute-start | bytes 12296 | tf_op jit(solution)/shard_map/cond/branch_5_fun/ppermute | solution.py:22
  72.6 4.0 %collective-permute-start.115 = (f32[136,128]{1,0:T(8,128)S(1)}, f32[136,128]{1,0:T(8,128)S(1)}, u32[]{:S(2)}, u32[]{:S(2)}) collective-permute-start(f32[136,128]{1,0:T(8,128)S(1)} %maximum_maximum_fusion.1), channel_id=1, source_target_pairs={{0,1},{1,0},{2,3},{3,2},{4,5},{5,4},{6,7},{7,6},{8,9},{9,8},{10,11... | collective-permute-start | bytes 208904 | tf_op jit(solution)/shard_map/ppermute | solution.py:22
  72.6 4.6 %collective-permute-start.116 = (f32[136,128]{1,0:T(8,128)S(1)}, f32[136,128]{1,0:T(8,128)S(1)}, u32[]{:S(2)}, u32[]{:S(2)}) collective-permute-start(f32[136,128]{1,0:T(8,128)S(1)} %maximum_maximum_fusion.1), channel_id=1, source_target_pairs={{0,2},{1,3},{2,0},{3,1},{4,6},{5,7},{6,4},{7,5},{8,10},{9,11},{10,... | collective-permute-start | bytes 208904 | tf_op jit(solution)/shard_map/ppermute | solution.py:22
  74.2 4.1 %collective-permute-start.117 = (f32[136,128]{1,0:T(8,128)S(1)}, f32[136,128]{1,0:T(8,128)S(1)}, u32[]{:S(2)}, u32[]{:S(2)}) collective-permute-start(f32[136,128]{1,0:T(8,128)S(1)} %maximum_maximum_fusion.1), channel_id=1, source_target_pairs={{0,3},{1,2},{2,1},{3,0},{4,7},{5,6},{6,5},{7,4},{8,11},{9,10},{10,... | collective-permute-start | bytes 208904 | tf_op jit(solution)/shard_map/ppermute | solution.py:22
  80.4 3.7 %collective-permute-start.50 = (f32[8,128]{1,0:T(8,128)S(1)}, f32[8,128]{1,0:T(8,128)S(1)}, u32[]{:S(2)}, u32[]{:S(2)}) collective-permute-start(f32[8,128]{1,0:T(8,128)S(1)} %broadcast_in_dim.55), channel_id=1, source_target_pairs={{0,4},{4,0},{8,12},{12,8},{16,20},{20,16},{24,28},{28,24},{1,5},{5... | collective-permute-start | bytes 12296 | tf_op jit(solution)/shard_map/cond/branch_3_fun/ppermute | solution.py:22
  84.7 4.8 %collective-permute-start.51 = (f32[8,128]{1,0:T(8,128)S(1)}, f32[8,128]{1,0:T(8,128)S(1)}, u32[]{:S(2)}, u32[]{:S(2)}) collective-permute-start(f32[8,128]{1,0:T(8,128)S(1)} %broadcast_maximum_fusion.10), channel_id=1, source_target_pairs={{0,8},{4,12},{8,0},{12,4},{16,24},{20,28},{24,16},{28,20},{1,9},{5... | collective-permute-start | bytes 12296 | tf_op jit(solution)/shard_map/cond/branch_3_fun/ppermute | solution.py:22
  86.5 31.2 %collective-permute-start.54 = (f32[128,128]{1,0:T(8,128)S(1)}, f32[128,128]{1,0:T(8,128)S(1)}, u32[]{:S(2)}, u32[]{:S(2)}) collective-permute-start(f32[128,128]{1,0:T(8,128)S(1)} %get-tuple-element.341), channel_id=1, source_target_pairs={{0,16},{4,20},{8,24},{12,28},{16,0},{20,4},{24,8},{28,12},{1,17},{... | collective-permute-start | bytes 196616 | tf_op jit(solution)/shard_map/cond/branch_3_fun/ppermute | solution.py:18
  88.2 30.9 %collective-permute-start.53 = (f32[1024,128]{1,0:T(8,128)S(1)}, f32[1024,128]{1,0:T(8,128)}, u32[]{:S(2)}, u32[]{:S(2)}) collective-permute-start(f32[1024,128]{1,0:T(8,128)S(1)} %add.373), channel_id=1, source_target_pairs={{0,16},{4,20},{8,24},{12,28},{16,0},{20,4},{24,8},{28,12},{1,17},{... | collective-permute-start | bytes 1572872 | tf_op jit(solution)/shard_map/cond/branch_3_fun/ppermute | solution.py:18
  90.2 24.4 %collective-permute-start.52 = (f32[8,128]{1,0:T(8,128)S(1)}, f32[8,128]{1,0:T(8,128)S(1)}, u32[]{:S(2)}, u32[]{:S(2)}) collective-permute-start(f32[8,128]{1,0:T(8,128)S(1)} %fusion.1477), channel_id=1, source_target_pairs={{0,16},{4,20},{8,24},{12,28},{16,0},{20,4},{24,8},{28,12},{1,17},{... | collective-permute-start | bytes 12296 | tf_op jit(solution)/shard_map/cond/branch_3_fun/ppermute | solution.py:22
  131.1 3.9 %collective-permute-start.118 = (f32[136,128]{1,0:T(8,128)S(1)}, f32[136,128]{1,0:T(8,128)S(1)}, u32[]{:S(2)}, u32[]{:S(2)}) collective-permute-start(f32[136,128]{1,0:T(8,128)S(1)} %maximum_maximum_fusion.2), channel_id=1, source_target_pairs={{0,1},{1,0},{2,3},{3,2},{4,5},{5,4},{6,7},{7,6},{8,9},{9,8},{10,11... | collective-permute-start | bytes 208904 | tf_op jit(solution)/shard_map/ppermute | solution.py:22
  131.1 4.6 %collective-permute-start.119 = (f32[136,128]{1,0:T(8,128)S(1)}, f32[136,128]{1,0:T(8,128)S(1)}, u32[]{:S(2)}, u32[]{:S(2)}) collective-permute-start(f32[136,128]{1,0:T(8,128)S(1)} %maximum_maximum_fusion.2), channel_id=1, source_target_pairs={{0,2},{1,3},{2,0},{3,1},{4,6},{5,7},{6,4},{7,5},{8,10},{9,11},{10,... | collective-permute-start | bytes 208904 | tf_op jit(solution)/shard_map/ppermute | solution.py:22
  132.7 4.2 %collective-permute-start.120 = (f32[136,128]{1,0:T(8,128)S(1)}, f32[136,128]{1,0:T(8,128)S(1)}, u32[]{:S(2)}, u32[]{:S(2)}) collective-permute-start(f32[136,128]{1,0:T(8,128)S(1)} %maximum_maximum_fusion.2), channel_id=1, source_target_pairs={{0,3},{1,2},{2,1},{3,0},{4,7},{5,6},{6,5},{7,4},{8,11},{9,10},{10,... | collective-permute-start | bytes 208904 | tf_op jit(solution)/shard_map/ppermute | solution.py:22
  138.8 3.7 %collective-permute-start.85 = (f32[8,128]{1,0:T(8,128)S(1)}, f32[8,128]{1,0:T(8,128)S(1)}, u32[]{:S(2)}, u32[]{:S(2)}) collective-permute-start(f32[8,128]{1,0:T(8,128)S(1)} %broadcast_in_dim.62), channel_id=1, source_target_pairs={{0,4},{4,0},{8,12},{12,8},{16,20},{20,16},{24,28},{28,24},{1,5},{5... | collective-permute-start | bytes 12296 | tf_op jit(solution)/shard_map/cond/branch_3_fun/ppermute | solution.py:22
  143.1 3.7 %collective-permute-start.86 = (f32[8,128]{1,0:T(8,128)S(1)}, f32[8,128]{1,0:T(8,128)S(1)}, u32[]{:S(2)}, u32[]{:S(2)}) collective-permute-start(f32[8,128]{1,0:T(8,128)S(1)} %broadcast_maximum_fusion.17), channel_id=1, source_target_pairs={{0,8},{4,12},{8,0},{12,4},{16,24},{20,28},{24,16},{28,20},{1,9},{5... | collective-permute-start | bytes 12296 | tf_op jit(solution)/shard_map/cond/branch_3_fun/ppermute | solution.py:22
  143.2 31.7 %collective-permute-start.89 = (f32[128,128]{1,0:T(8,128)S(1)}, f32[128,128]{1,0:T(8,128)S(1)}, u32[]{:S(2)}, u32[]{:S(2)}) collective-permute-start(f32[128,128]{1,0:T(8,128)S(1)} %get-tuple-element.369), channel_id=1, source_target_pairs={{0,16},{4,20},{8,24},{12,28},{16,0},{20,4},{24,8},{28,12},{1,17},{... | collective-permute-start | bytes 196616 | tf_op jit(solution)/shard_map/cond/branch_3_fun/ppermute | solution.py:18
  146.2 30.0 %collective-permute-start.88 = (f32[1024,128]{1,0:T(8,128)S(1)}, f32[1024,128]{1,0:T(8,128)}, u32[]{:S(2)}, u32[]{:S(2)}) collective-permute-start(f32[1024,128]{1,0:T(8,128)S(1)} %add.401), channel_id=1, source_target_pairs={{0,16},{4,20},{8,24},{12,28},{16,0},{20,4},{24,8},{28,12},{1,17},{... | collective-permute-start | bytes 1572872 | tf_op jit(solution)/shard_map/cond/branch_3_fun/ppermute | solution.py:18
  147.4 24.4 %collective-permute-start.87 = (f32[8,128]{1,0:T(8,128)S(1)}, f32[8,128]{1,0:T(8,128)S(1)}, u32[]{:S(2)}, u32[]{:S(2)}) collective-permute-start(f32[8,128]{1,0:T(8,128)S(1)} %fusion.1484), channel_id=1, source_target_pairs={{0,16},{4,20},{8,24},{12,28},{16,0},{20,4},{24,8},{28,12},{1,17},{... | collective-permute-start | bytes 12296 | tf_op jit(solution)/shard_map/cond/branch_3_fun/ppermute | solution.py:22
